TPU v7x, 256 devices: a whole 4x4x8 slice. The times are simulated.
256 devices in a mesh: col: 16 (over z, core), row: 16 (over x, y).
Axes of the slice: x: 4, y: 4, z: 8, core: 2. Of those that a mesh axis runs over, the one named last changes fastest.
Arguments:
- top_sources: bfloat16 [14, 256, 256], P(None, 'row', 'col'), may hold values from -6 to 6
- leaf_sources: bfloat16 [2048, 256, 256], P(('col', 'row')), may hold values from -6 to 6
- top_inverse: bfloat16 [14, 256, 256], P(None, 'row'), may hold values from -1 to 4
- leaf_inverse: bfloat16 [2048, 256, 256], P(('col', 'row')), may hold values from -1 to 4
- top_coupling: bfloat16 [12, 6, 256, 256], P(None, None, 'row'), may hold values from -0.1875 to 0.1875
- leaf_coupling: bfloat16 [2048, 9, 256, 256], P(('col', 'row')), may hold values from -0.125 to 0.125
- leaf_links: int32 [2048, 9], P(('col', 'row')), may hold values from 0 to 13, as said below
Outputs:
- top_adjoint: bfloat16 [14, 256, 256], P(None, 'row', 'col')
- leaf_adjoint: bfloat16 [2048, 256, 256], P(('col', 'row'))
Inputs may be any that keep to these rules, and one draw needn't show every extreme that they name: `leaf_links`: entries 0 to 1 of a row name distinct blocks of level 0, the next 3 distinct blocks of level 1, the last 4 distinct blocks of level 2.
All inputs are finite; a program needn't handle non-finite values.
Results may differ from a plain program's by a relative error of at most 0.0072.
Values may be sent and summed in bfloat16 or wider, within the bound.
A program may use at most 128 MiB of HBM per device.

v0:
```python
from functools import partial

import jax
import jax.numpy as jnp
from jax import lax
from jax.sharding import PartitionSpec as P

LEVEL0 = 2
LEVEL1 = 4
LEVEL2 = 8
LINKS0 = 2
LINKS1 = 3
LINKS2 = 4


def leaf_terms(coupling, indices, block_piece):
    picked = jnp.take(block_piece, indices, axis=0)
    return jnp.einsum("iqrs,iqsc->irc", coupling, picked, preferred_element_type=jnp.float32)


def leaf_piece(coupling, indices, block_piece, piece_start):
    return leaf_terms(coupling, indices, block_piece)


def local(
    top_sources, leaf_sources, top_inverse, leaf_inverse, top_coupling, leaf_coupling, leaf_links
):
    local_rows = top_inverse.shape[1]
    block_starts = (0, LEVEL0, LEVEL0 + LEVEL1)
    block_counts = (LEVEL0, LEVEL1, LEVEL2)
    link_starts = (0, LINKS0, LINKS0 + LINKS1)
    link_counts = (LINKS0, LINKS1, LINKS2)
    source_width = top_sources.shape[2]
    solved = []
    leaf_update = jnp.zeros(leaf_sources.shape, jnp.float32)
    for tree_level in range(3):
        start_block = block_starts[tree_level]
        stop_block = start_block + block_counts[tree_level]
        update = jnp.zeros((block_counts[tree_level], local_rows, source_width), jnp.float32)
        for earlier in range(tree_level):
            prior_start = block_starts[earlier]
            prior_stop = prior_start + block_counts[earlier]
            coupling_top = top_coupling[
                start_block - LEVEL0 : stop_block - LEVEL0, prior_start:prior_stop
            ]
            update = update + jnp.einsum(
                "jbrs,bsc->jrc", coupling_top, solved[earlier], preferred_element_type=jnp.float32
            )
        residual = (top_sources[start_block:stop_block].astype(jnp.float32) - update).astype(
            jnp.bfloat16
        )
        gathered = lax.all_gather(residual, "row", axis=1, tiled=True)
        own_rows = jnp.einsum(
            "jrs,jsc->jrc",
            top_inverse[start_block:stop_block],
            gathered,
            preferred_element_type=jnp.float32,
        ).astype(jnp.bfloat16)
        adjoint = lax.all_gather(own_rows, "row", axis=1, tiled=True)
        solved.append(adjoint)
        link_first = link_starts[tree_level]
        link_stop = link_first + link_counts[tree_level]
        coupling = leaf_coupling[:, link_first:link_stop]
        indices = leaf_links[:, link_first:link_stop] - start_block
        leaf_feed = partial(leaf_piece, coupling, indices)
        leaf_update = leaf_update + leaf_feed(
            lax.all_gather(adjoint, "col", axis=2, tiled=True), jnp.int32(0)
        )
    leaf_residual = (leaf_sources.astype(jnp.float32) - leaf_update).astype(jnp.bfloat16)
    leaf_adjoint = jnp.einsum(
        "irs,isc->irc", leaf_inverse, leaf_residual, preferred_element_type=jnp.float32
    ).astype(jnp.bfloat16)
    stacked = jnp.concatenate(solved, axis=0)
    top_adjoint = lax.dynamic_slice_in_dim(
        stacked, lax.axis_index("row") * local_rows, local_rows, 1
    )
    return (top_adjoint, leaf_adjoint)


def solution(mesh):
    in_specs = (
        P(None, "row", "col"),
        P(("col", "row"), None, None),
        P(None, "row", None),
        P(("col", "row"), None, None),
        P(None, None, "row", None),
        P(("col", "row"), None, None, None),
        P(("col", "row"), None),
    )
    out_specs = (P(None, "row", "col"), P(("col", "row"), None, None))
    return jax.shard_map(local, mesh=mesh, in_specs=in_specs, out_specs=out_specs, check_vma=False)
```

profile of v0, /device:TPU:1, one launch (start us, length us, event | category | flops | bytes accessed | tf_op | source)
XLA Modules:
  0.0 239.8 jit_solution(2995232696490618794)
XLA Ops:
  7.2 0.0 copy-start
  7.2 0.0 slice-start
  7.2 0.0 all-gather.2.cloned.1.call-start
  7.2 0.8 slice.46
  8.0 0.7 slice.47
  8.7 1.0 slice.52
  9.7 0.9 slice.51
  10.6 19.4 %all_gather.27 = bf16[2,256,16]{2,1,0:T(8,128)(2,1)S(1)} all-gather(bf16[2,16,16]{2,1,0:T(8,128)(2,1)S(1)} %slice.46), channel_id=1, replica_groups=mesh['col'=16,'row'=16] {'row'}, dimensions={1}, use_global_device_ids=true | all-gather | bytes 17408 | tf_op jit(solution)/shard_map/all_gather | solution.py:52
  30.0 0.0 copy-start.4
  30.0 0.9 convolution_convert_fusion.3
  30.9 17.7 %all_gather.28 = bf16[2,256,16]{2,1,0:T(8,128)(2,1)S(1)} all-gather(bf16[2,16,16]{2,1,0:T(8,128)(2,1)S(1)} %convolution_convert_fusion.3), channel_id=1, replica_groups=mesh['col'=16,'row'=16] {'row'}, dimensions={1}, use_global_device_ids=true | all-gather | bytes 17408 | tf_op jit(solution)/shard_map/all_gather | solution.py:59
  48.6 0.1 copy.83
  48.7 1.0 fusion.30
  49.8 0.1 copy.50
  49.9 16.5 %all_gather.29 = bf16[4,256,16]{2,0,1:T(4,128)(2,1)S(1)} all-gather(bf16[4,16,16]{2,0,1:T(4,128)(2,1)S(1)} %copy.50), channel_id=1, replica_groups=mesh['col'=16,'row'=16] {'row'}, dimensions={1}, use_global_device_ids=true | all-gather | bytes 34816 | tf_op jit(solution)/shard_map/all_gather | solution.py:52
  66.3 1.0 fusion.31
  67.3 0.1 copy.52
  67.4 17.5 %all_gather.30 = bf16[4,256,16]{2,0,1:T(4,128)(2,1)S(1)} all-gather(bf16[4,16,16]{2,0,1:T(4,128)(2,1)S(1)} %copy.52), channel_id=1, replica_groups=mesh['col'=16,'row'=16] {'row'}, dimensions={1}, use_global_device_ids=true | all-gather | bytes 34816 | tf_op jit(solution)/shard_map/all_gather | solution.py:59
  85.0 0.3 convolution_bitcast_fusion.1
  85.2 0.0 slice-done
  85.3 0.0 copy-start.3
  85.3 0.2 fusion.27
  85.5 16.8 %all_gather.31 = bf16[8,256,16]{2,0,1:T(8,128)(2,1)S(1)} all-gather(bf16[8,16,16]{2,0,1:T(8,128)(2,1)S(1)} %fusion.27), channel_id=1, replica_groups=mesh['col'=16,'row'=16] {'row'}, dimensions={1}, use_global_device_ids=true | all-gather | bytes 69632 | tf_op jit(solution)/shard_map/all_gather | solution.py:52
  102.3 0.0 copy-done.4
  102.3 0.3 fusion.28
  102.5 0.1 copy.58
  102.7 17.8 %all_gather.32 = bf16[8,256,16]{2,0,1:T(8,128)(2,1)S(1)} all-gather(bf16[8,16,16]{2,0,1:T(8,128)(2,1)S(1)} %copy.58), channel_id=1, replica_groups=mesh['col'=16,'row'=16] {'row'}, dimensions={1}, use_global_device_ids=true | all-gather | bytes 69632 | tf_op jit(solution)/shard_map/all_gather | solution.py:59
  120.4 1.0 copy.69
  121.4 0.0 all-gather.2.cloned.1.call-update
  121.4 0.3 copy.61
  121.7 0.1 copy.60
  121.9 0.1 copy.59
  122.0 0.2 copy.66
  122.1 0.1 copy.63
  122.2 0.1 fusion.44
  122.3 0.7 copy.72
  123.1 0.0 copy-done.3
  123.1 0.1 compare_select_fusion
  123.1 0.1 reshape.37
  123.2 55.2 %all_gather.34 = bf16[4,256,256]{1,0,2:T(4,128)(2,1)S(1)} all-gather(bf16[4,256,16]{1,0,2:T(4,128)(2,1)S(1)} %copy.66), channel_id=1, replica_groups=mesh['col'=16,'row'=16] {'col'}, dimensions={2}, use_global_device_ids=true | all-gather | bytes 557056 | tf_op jit(solution)/shard_map/all_gather | solution.py:67
  178.5 0.3 copy.67
  178.8 0.1 compare_select_fusion.1
  178.9 0.1 reshape.29
  179.0 15.3 %all_gather.33 = bf16[2,256,256]{1,0,2:T(2,128)(2,1)S(1)} all-gather(bf16[2,256,16]{1,0,2:T(2,128)(2,1)S(1)} %copy.63), channel_id=1, replica_groups=mesh['col'=16,'row'=16] {'col'}, dimensions={2}, use_global_device_ids=true | all-gather | bytes 278528 | tf_op jit(solution)/shard_map/all_gather | solution.py:67
  194.2 0.2 copy.64
  194.4 0.1 reshape.21
  194.5 2.0 gather_fusion
  196.5 0.0 copy-start.1
  196.5 4.0 %copy.65 = bf16[8,2,256,256]{2,3,1,0:T(8,128)(2,1)} copy(bf16[8,2,256,256]{3,2,1,0:T(8,128)(2,1)} %bitcast.76) | data formatting | bytes 4194304 | tf_op jit(solution)/shard_map/jit(_take)/gather | solution.py:17
  200.5 0.0 copy-done.1
  200.5 1.3 copy.62
  201.8 2.6 %gather_fusion.1 = bf16[24,256,256]{2,1,0:T(8,128)(2,1)} fusion(bf16[4,256,256]{2,1,0:T(8,128)(2,1)S(1)} %copy.67, s32[1024]{0:T(1024)S(1)} %pad_clamp_fusion.1), kind=kCustom, calls=%fused_computation.1 | custom fusion | bytes 6291552 | tf_op jit(solution)/shard_map/jit(_take)/gather | solution.py:17
  204.4 0.1 compare_and_fusion
  204.5 0.1 compare_and_fusion.1
  204.6 4.4 %fusion.10 = f32[8,256,256,1]{2,1,3,0:T(8,128)} fusion(bf16[8,9,256,256]{3,2,1,0:T(8,128)(2,1)} %param.12, bf16[8,2,256,256]{2,3,1,0:T(8,128)(2,1)} %copy.65, pred[8,2]{1,0:T(8,128)(4,1)S(1)} %compare_and_fusion.2), kind=kOutput, calls=%fused_computation.16 | convolution fusion | flops 537919488 | bytes 6291472 | tf_op jit(solution)/shard_map/iqrs,iqsc->irc/dot_general | solution.py:18
  209.0 1.6 copy.70
  210.6 2.8 %gather_fusion.2 = bf16[32,256,256]{2,1,0:T(8,128)(2,1)} fusion(bf16[8,256,256]{2,1,0:T(8,128)(2,1)S(1)} %copy.70, s32[1024]{0:T(1024)S(1)} %pad_clamp_fusion), kind=kCustom, calls=%fused_computation.2 | custom fusion | bytes 8388736 | tf_op jit(solution)/shard_map/jit(_take)/gather | solution.py:17
  213.4 6.4 %copy.71 = bf16[8,4,256,256]{2,3,1,0:T(8,128)(2,1)} copy(bf16[8,4,256,256]{3,2,1,0:T(8,128)(2,1)} %bitcast.75) | data formatting | bytes 8388608 | tf_op jit(solution)/shard_map/jit(_take)/gather | solution.py:17
  219.8 0.0 copy-start.2
  219.8 6.2 %fusion = f32[8,256,256,1]{2,1,3,0:T(8,128)} fusion(bf16[8,9,256,256]{3,2,1,0:T(8,128)(2,1)} %param.12, bf16[8,4,256,256]{2,3,1,0:T(8,128)(2,1)} %copy.71, pred[8,4]{1,0:T(8,128)(4,1)S(1)} %compare_and_fusion), kind=kOutput, calls=%fused_computation.3 | convolution fusion | flops 1075838976 | bytes 10485792 | tf_op jit(solution)/shard_map/iqrs,iqsc->irc/dot_general | solution.py:18
  226.0 0.0 copy-done
  226.0 0.0 copy-done.2
  226.0 5.7 %fusion.19 = bf16[8,256,256]{1,2,0:T(8,128)(2,1)S(1)} fusion(bf16[8,256,256]{2,1,0:T(8,128)(2,1)S(1)} %copy-done, f32[8,256,256,1]{2,1,3,0:T(8,128)} %fusion, f32[8,256,256,1]{2,1,3,0:T(8,128)} %fusion.10, bf16[8,256,256]{1,2,0:T(8,128)(2,1)S(1)} %copy-done.2, bf16[8,9,256,256]{3,2,1,0:T(8,128)(2,1)} %param.12, bf16[8,3,256,256]{3,2,1,0:T(8,128)(2,1)} %bitcast.77, ...), kind=kOutput, calls=%fused_computation.22 | convolution fusion | flops 1078460416 | bytes 13631512 | tf_op jit(solution)/shard_map/irs,isc->irc/dot_general | solution.py:70
  231.7 1.3 copy.73
  (6 shorter events, 0.0 us)
Async XLA Ops:
  7.2 218.8 %copy-start = (bf16[8,256,256]{2,1,0:T(8,128)(2,1)S(1)}, bf16[8,256,256]{2,1,0:T(8,128)(2,1)}, u32[]{:S(2)}) copy-start(bf16[8,256,256]{2,1,0:T(8,128)(2,1)} %param.10) | copy-start | bytes 3145732
  7.2 78.1 %slice-start = ((bf16[14,16,16]{2,1,0:T(8,128)(2,1)}), bf16[8,16,16]{2,1,0:T(8,128)(2,1)S(1)}, s32[]{:S(2)}) async-start(bf16[14,16,16]{2,1,0:T(8,128)(2,1)} %param.7), calls=%async_computation.1 | async-start | bytes 65536 | tf_op jit(solution)/shard_map/slice | solution.py:49
  7.2 201.8 %all-gather.2.cloned.1.call-start = ((), (), s32[]{:S(2)}) async-start(), calls=%async_computation | async-start | bytes 1114112 | tf_op jit(solution)/shard_map/all_gather | solution.py:67
  30.0 72.3 %copy-start.4 = (bf16[14,16,256]{2,1,0:T(8,128)(2,1)S(1)}, bf16[14,16,256]{2,1,0:T(8,128)(2,1)}, u32[]{:S(2)}) copy-start(bf16[14,16,256]{2,1,0:T(8,128)(2,1)} %param.9) | copy-start | bytes 344068
  85.3 37.8 %copy-start.3 = (s32[8,9]{1,0:T(8,128)S(1)}, s32[8,9]{1,0:T(8,128)}, u32[]{:S(2)}) copy-start(s32[8,9]{1,0:T(8,128)} %param.13) | copy-start | bytes 868
  196.5 4.0 %copy-start.1 = (bf16[8,256,256]{2,1,0:T(8,128)(2,1)S(1)}, bf16[8,256,256]{2,1,0:T(8,128)(2,1)}, u32[]{:S(2)}) copy-start(bf16[8,256,256]{2,1,0:T(8,128)(2,1)} %param.8) | copy-start | bytes 3145732
  219.8 6.2 %copy-start.2 = (bf16[8,256,256]{1,2,0:T(8,128)(2,1)S(1)}, bf16[8,256,256]{1,2,0:T(8,128)(2,1)}, u32[]{:S(2)}) copy-start(bf16[8,256,256]{1,2,0:T(8,128)(2,1)} %copy.62) | copy-start | bytes 3145732
Sparse Core Ops, SparseCore 0:
  121.5 71.1 all-gather.1
where the time goes:
time: 241 us; the launch traced here: 240 us
  blocking collectives  176 us (73%)
  local copies, waits for them, and re-layouts  29.1 us (12%)
  matrix products  19.9 us (8%)
  between operations  14.2 us (6%)
    all_gather x2, blocking collectives, local(): lax.all_gather(adjoint, 'col', axis=2, tiled=True)  70.5 us
    all_gather x3, blocking collectives, local(): adjoint = lax.all_gather(own_rows, 'row', axis=1, tiled=True)  53 us
    all_gather x3, blocking collectives, local(): gathered = lax.all_gather(residual, 'row', axis=1, tiled=True)  52.6 us
    gather x5, local copies, waits for them, and re-layouts, leaf_terms(): picked = jnp.take(block_piece, indices, axis=0)  17.8 us
    dot_general x2, matrix products, leaf_terms(): jnp.einsum('iqrs,iqsc->irc', coupling, picked, preferred_element_type=jnp...  10.6 us
    dot_general x1, matrix products, local(): jnp.einsum('irs,isc->irc', leaf_inverse, leaf_residual, preferred_element...  5.68 us
  transfers between devices with their start and end apart: 1, of which 0 were waited for; matrix products, arithmetic and copies ran while one was open for 7% of the time, Pallas kernels for 0%

commit v1 on v0

v1 whole, which is shorter than its diff:
```python
import jax
import jax.numpy as jnp
from jax import lax
from jax.experimental import pallas as pl
from jax.experimental.pallas import tpu as pltpu
from jax.sharding import PartitionSpec as P

LEVEL0 = 2
LEVEL1 = 4
LEVEL2 = 8
EARLY = LEVEL0 + LEVEL1
TOP = EARLY + LEVEL2
EARLY_LINKS = 5
LINKS = 9
LEAVES = 8
BLOCK = 256
HALF = 128
ROWS = 16
WIDTH = 16
PLANE = 16
DEPTH = 8
MESH = pl.DeviceIdType.MESH
BF16 = jnp.bfloat16
F32 = jnp.float32


def dot(a, b):
    return jnp.dot(a, b, preferred_element_type=F32)


def kernel(
    links,
    top_sources,
    leaf_sources,
    top_inverse,
    leaf_inverse,
    top_coupling,
    leaf_coupling,
    top_out,
    leaf_out,
    src_own,
    pack,
    zbuf,
    src_rows,
    sources,
    inv0,
    inv1,
    inv2,
    coup1,
    coup2,
    early,
    late,
    res_rows,
    residual,
    coupling,
    inverse,
    leaf_src,
    update,
    leaf_res,
    top_res,
    local_sem,
    send_sem,
    recv_sem,
    core_send,
    core_recv,
    leaf_sem,
    out_sem,
):
    col, row = lax.axis_index("col"), lax.axis_index("row")
    z, k = col // 2, lax.rem(col, 2)
    own = pl.multiple_of(row * ROWS, ROWS)
    rows = pl.ds(own, ROWS)
    other = (z * 2 + 1 - k, row)

    def row_peer(d):
        return (col, lax.rem(row + d, PLANE))

    first = pltpu.make_async_copy(top_sources, src_own, local_sem.at[0])
    first.start()
    barrier = pltpu.get_barrier_semaphore()

    def greet(d, carry):
        pl.semaphore_signal(barrier, 1, device_id=row_peer(d), device_id_type=MESH)
        pl.semaphore_signal(
            barrier, 1, device_id=(lax.rem(col + d, PLANE), row), device_id_type=MESH
        )
        return carry

    lax.fori_loop(1, PLANE, greet, 0)
    second = pltpu.make_async_copy(top_coupling.at[pl.ds(LEVEL1, LEVEL2)], coup2, local_sem.at[1])
    second.start()

    half0 = pl.ds(k, 1)
    half1 = pl.ds(LEVEL0 + 2 * k, 2)
    half2 = pl.ds(EARLY + 4 * k, 4)
    pairs = pl.ds(2 * k, 2)
    early_pairs = pl.ds(0, LEVEL0)
    groups = (
        (top_inverse.at[half0], lambda at: inv0.at[half0, at]),
        (
            top_coupling.at[pairs, early_pairs],
            lambda at: coup1.at[pairs, :, at],
        ),
        (top_inverse.at[half1], lambda at: inv1.at[pairs, at]),
        (top_inverse.at[half2], lambda at: inv2.at[pl.ds(4 * k, 4), at]),
    )
    for g, (source, place) in enumerate(groups):
        pltpu.make_async_copy(source, place(rows), recv_sem.at[g]).start()

    first.wait()
    lane = lax.broadcasted_iota(jnp.int32, (WIDTH, BLOCK), 1)
    repeat = (lax.rem(lane, WIDTH) == lax.broadcasted_iota(jnp.int32, (WIDTH, BLOCK), 0)).astype(
        F32
    ).astype(BF16)
    spread = dot(src_own[...].reshape(TOP * ROWS, WIDTH), repeat)
    place_row = lax.broadcasted_iota(jnp.int32, (TOP * ROWS, BLOCK), 0) // ROWS
    place_lane = lax.broadcasted_iota(jnp.int32, (TOP * ROWS, BLOCK), 1) // WIDTH
    spread = jnp.where(place_row == place_lane, spread, 0.0)
    pack[...] = spread.reshape(TOP, ROWS, BLOCK).sum(axis=0).astype(BF16)

    pl.semaphore_wait(barrier, 2 * (PLANE - 1))

    zhalf = z // 4
    slot = lax.rem(col, 8)

    def send_z(d, carry):
        pltpu.make_async_remote_copy(
            src_ref=pack,
            dst_ref=zbuf.at[slot],
            send_sem=send_sem.at[4],
            recv_sem=recv_sem.at[4],
            device_id=(lax.rem(z + d, DEPTH) * 2 + zhalf, row),
            device_id_type=MESH,
        ).start()
        return carry

    @pl.when(k == zhalf)
    def _():
        pltpu.make_async_copy(pack, zbuf.at[slot], recv_sem.at[4]).start()

    @pl.when(k != zhalf)
    def _():
        pltpu.make_async_remote_copy(
            src_ref=pack,
            dst_ref=zbuf.at[slot],
            send_sem=send_sem.at[7],
            recv_sem=recv_sem.at[4],
            device_id=other,
            device_id_type=MESH,
        ).start()

    lax.fori_loop(1, DEPTH, send_z, 0)

    def gather(g, source, target):
        def send(d, carry):
            pltpu.make_async_remote_copy(
                src_ref=source,
                dst_ref=target,
                send_sem=send_sem.at[g],
                recv_sem=recv_sem.at[g],
                device_id=row_peer(d),
                device_id_type=MESH,
            ).start()
            return carry

        lax.fori_loop(1, PLANE, send, 0)

    for g in range(3):
        gather(g, groups[g][0], groups[g][1](rows))

    leaf_copies = (
        pltpu.make_async_copy(leaf_sources, leaf_src, leaf_sem.at[0]),
        pltpu.make_async_copy(leaf_coupling, coupling, leaf_sem.at[1]),
        pltpu.make_async_copy(leaf_inverse, inverse, leaf_sem.at[2]),
    )
    for copy in leaf_copies:
        copy.start()

    pltpu.make_async_copy(zbuf, zbuf, recv_sem.at[4]).wait()
    square = (HALF, HALF)
    from_lane = lax.broadcasted_iota(jnp.int32, square, 0)
    to_lane = lax.broadcasted_iota(jnp.int32, square, 1)
    keep = from_lane // ROWS == to_lane // WIDTH
    collected = zbuf[...].reshape(HALF, BLOCK)
    for j in range(TOP):
        pick = (from_lane == lax.rem(to_lane, WIDTH) + WIDTH * (j % 8)).astype(F32).astype(BF16)
        moved = dot(collected[:, HALF * (j // 8) : HALF * (j // 8 + 1)], pick)
        moved = jnp.where(keep, moved, 0.0).reshape(DEPTH, ROWS, HALF).sum(axis=0).astype(BF16)
        src_rows[j] = moved
    early_rows = src_rows.at[pl.ds(0, EARLY)]
    pltpu.make_async_copy(early_rows, sources.at[:, rows], recv_sem.at[5]).start()
    gather(5, early_rows, sources.at[:, rows])
    gather(3, groups[3][0], groups[3][1](rows))

    halves = (
        inv0.at[half0],
        coup1.at[pairs],
        inv1.at[pairs],
        inv2.at[pl.ds(4 * k, 4)],
    )

    def share(g, part):
        copy = pltpu.make_async_remote_copy(
            src_ref=part,
            dst_ref=part,
            send_sem=core_send.at[g],
            recv_sem=core_recv.at[g],
            device_id=other,
            device_id_type=MESH,
        )
        copy.start()
        return copy

    shared = []
    for g in range(3):
        pltpu.make_async_copy(halves[g], halves[g], recv_sem.at[g]).wait()
        shared.append(share(g, halves[g]))

    shared[0].wait_recv()
    pltpu.make_async_copy(sources, sources, recv_sem.at[5]).wait()
    for b in range(LEVEL0):
        early[k, b] = dot(inv0[b], sources[b]).astype(BF16)
    shared[1].wait_recv()
    shared[2].wait_recv()
    for j in range(LEVEL1):
        total = dot(coup1[j, 0], early[k, 0]) + dot(coup1[j, 1], early[k, 1])
        rest = (sources[LEVEL0 + j].astype(F32) - total).astype(BF16)
        early[k, LEVEL0 + j] = dot(inv1[j], rest).astype(BF16)

    second.wait()
    total = jnp.zeros((LEVEL2 * ROWS, HALF), F32)
    for b in range(EARLY):
        total = total + dot(coup2[:, b].reshape(LEVEL2 * ROWS, BLOCK), early[k, b])
    late_src = src_rows[pl.ds(EARLY, LEVEL2)].astype(F32)
    res_rows[...] = (late_src - total.reshape(LEVEL2, ROWS, HALF)).astype(BF16)
    pltpu.make_async_copy(res_rows, residual.at[:, rows], recv_sem.at[6]).start()
    gather(6, res_rows, residual.at[:, rows])
    shared.append(share(4, early.at[k]))
    pltpu.make_async_copy(halves[3], halves[3], recv_sem.at[3]).wait()
    shared.append(share(3, halves[3]))

    shared[3].wait_recv()
    for copy in leaf_copies:
        copy.wait()

    def early_leaf(i, carry):
        total = leaf_src[i].astype(F32)
        for q in range(EARLY_LINKS):
            at = links[i, q]
            picked = jnp.concatenate([early[0, at], early[1, at]], axis=1)
            total = total - dot(coupling[i, q], picked)
        update[i] = total
        return carry

    lax.fori_loop(0, LEAVES, early_leaf, 0)

    shared[4].wait_recv()
    pltpu.make_async_copy(residual, residual, recv_sem.at[6]).wait()
    for part in range(2):
        for j in range(4 * part, 4 * part + 4):
            late[k, j] = dot(inv2[j], residual[j]).astype(BF16)
        shared.append(share(5 + part, late.at[k, pl.ds(4 * part, 4)]))
    shared[5].wait_recv()
    shared[6].wait_recv()

    def late_leaf(i, carry):
        total = update[i]
        for q in range(EARLY_LINKS, LINKS):
            at = jnp.maximum(links[i, q] - EARLY, 0)
            picked = jnp.concatenate([late[0, at], late[1, at]], axis=1)
            total = total - dot(coupling[i, q], picked)
        leaf_res[i] = dot(inverse[i], total.astype(BF16)).astype(BF16)
        pltpu.make_async_copy(leaf_res.at[i], leaf_out.at[i], out_sem.at[0]).start()
        return carry

    lax.fori_loop(0, LEAVES, late_leaf, 0)

    from_lane = lax.broadcasted_iota(jnp.int32, (HALF, WIDTH), 0)
    to_lane = lax.broadcasted_iota(jnp.int32, (HALF, WIDTH), 1)
    pick = (from_lane == to_lane + WIDTH * slot).astype(F32).astype(BF16)
    mine = early[zhalf, :, rows].reshape(EARLY * ROWS, HALF)
    top_res[pl.ds(0, EARLY)] = dot(mine, pick).astype(BF16).reshape(EARLY, ROWS, WIDTH)
    mine = late[zhalf, :, rows].reshape(LEVEL2 * ROWS, HALF)
    top_res[pl.ds(EARLY, LEVEL2)] = dot(mine, pick).astype(BF16).reshape(LEVEL2, ROWS, WIDTH)
    last = pltpu.make_async_copy(top_res, top_out, out_sem.at[1])
    last.start()

    for copy in shared:
        copy.wait_send()
    others = pl.ds(0, BLOCK - ROWS)
    sent = (
        inv0.at[half0, others],
        coup1.at[pairs, :, others],
        inv1.at[pairs, others],
        inv2.at[pl.ds(4 * k, 4), others],
        zbuf.at[pl.ds(0, DEPTH - 1)],
        sources.at[:, others],
        residual.at[:, others],
    )
    for g, part in enumerate(sent):
        pltpu.make_async_copy(part, part, send_sem.at[g]).wait()

    @pl.when(k != zhalf)
    def _():
        pltpu.make_async_copy(pack, pack, send_sem.at[7]).wait()

    pltpu.make_async_copy(leaf_res, leaf_out, out_sem.at[0]).wait()
    last.wait()


def local(
    top_sources, leaf_sources, top_inverse, leaf_inverse, top_coupling, leaf_coupling, leaf_links
):
    anywhere = pl.BlockSpec(memory_space=pl.ANY)
    vmem, dma = pltpu.VMEM, pltpu.SemaphoreType.DMA
    return pl.pallas_call(
        kernel,
        out_shape=(
            jax.ShapeDtypeStruct((TOP, ROWS, WIDTH), BF16),
            jax.ShapeDtypeStruct((LEAVES, BLOCK, BLOCK), BF16),
        ),
        in_specs=[pl.BlockSpec(memory_space=pltpu.SMEM)] + [anywhere] * 6,
        out_specs=(anywhere, anywhere),
        scratch_shapes=[
            vmem((TOP, ROWS, WIDTH), BF16),
            vmem((ROWS, BLOCK), BF16),
            vmem((DEPTH, ROWS, BLOCK), BF16),
            vmem((TOP, ROWS, HALF), BF16),
            vmem((EARLY, BLOCK, HALF), BF16),
            vmem((LEVEL0, BLOCK, BLOCK), BF16),
            vmem((LEVEL1, BLOCK, BLOCK), BF16),
            vmem((LEVEL2, BLOCK, BLOCK), BF16),
            vmem((LEVEL1, LEVEL0, BLOCK, BLOCK), BF16),
            vmem((LEVEL2, EARLY, ROWS, BLOCK), BF16),
            vmem((2, EARLY, BLOCK, HALF), BF16),
            vmem((2, LEVEL2, BLOCK, HALF), BF16),
            vmem((LEVEL2, ROWS, HALF), BF16),
            vmem((LEVEL2, BLOCK, HALF), BF16),
            vmem((LEAVES, LINKS, BLOCK, BLOCK), BF16),
            vmem((LEAVES, BLOCK, BLOCK), BF16),
            vmem((LEAVES, BLOCK, BLOCK), BF16),
            vmem((LEAVES, BLOCK, BLOCK), F32),
            vmem((LEAVES, BLOCK, BLOCK), BF16),
            vmem((TOP, ROWS, WIDTH), BF16),
            dma((2,)),
            dma((8,)),
            dma((7,)),
            dma((7,)),
            dma((7,)),
            dma((3,)),
            dma((2,)),
        ],
        compiler_params=pltpu.CompilerParams(
            collective_id=0, has_side_effects=True, vmem_limit_bytes=56 * 2**20
        ),
    )(
        leaf_links,
        top_sources,
        leaf_sources,
        top_inverse,
        leaf_inverse,
        top_coupling,
        leaf_coupling,
    )


def solution(mesh):
    in_specs = (
        P(None, "row", "col"),
        P(("col", "row"), None, None),
        P(None, "row", None),
        P(("col", "row"), None, None),
        P(None, None, "row", None),
        P(("col", "row"), None, None, None),
        P(("col", "row"), None),
    )
    out_specs = (P(None, "row", "col"), P(("col", "row"), None, None))
    return jax.shard_map(local, mesh=mesh, in_specs=in_specs, out_specs=out_specs, check_vma=False)
```

time: 241 us -> 53.9 us (0.22)
  blocking collectives: 176 us -> 0 us
  Pallas kernels: 0 us -> 48.7 us
  local copies, waits for them, and re-layouts: 29.1 us -> 3.71 us
  matrix products: 19.9 us -> 0 us
  between operations: 14.2 us -> 0.64 us
    all_gather x8 -> x0, blocking collectives: 176 us -> none  [the longest x2 70.5 us: local(): lax.all_gather(adjoint, 'col', axis=2, tiled=True)]
    pallas_call x0 -> x1, Pallas kernels: none -> 48.7 us  [local(): pl.pallas_call(kernel, out_shape=(jax.ShapeDtypeStruct((TOP, ROWS, WIDTH)...]
    dot_general x9 -> x0, matrix products: 19.9 us -> none  [the longest x2 10.6 us: leaf_terms(): jnp.einsum('iqrs,iqsc->irc', coupling, picked, preferred_element_type=jnp...]
    gather x5 -> x0, local copies, waits for them, and re-layouts: 17.8 us -> none  [leaf_terms(): picked = jnp.take(block_piece, indices, axis=0)]
    all_gather x9 -> x0, local copies, waits for them, and re-layouts: 3.9 us -> none  [the longest x3 2.13 us: local(): lax.all_gather(adjoint, 'col', axis=2, tiled=True)]
    slice x6 -> x0, local copies, waits for them, and re-layouts: 3.39 us -> none  [the longest x2 1.89 us: local(): top_coupling[start_block - LEVEL0:stop_block - LEVEL0, prior_start:prior_...]
  transfers between devices with their start and end apart: 1 -> 0, of which waited for: 0 -> 0; matrix products, arithmetic and copies ran while one was open for 7% -> 0% of each run, Pallas kernels for 0% -> 0%
where the time goes in v1:
time: 53.9 us; the launch traced here: 53.1 us
  Pallas kernels  48.7 us (90%)
  local copies, waits for them, and re-layouts  3.71 us (7%)
  between operations  0.64 us (1%)
    pallas_call x1, Pallas kernels, local(): pl.pallas_call(kernel, out_shape=(jax.ShapeDtypeStruct((TOP, ROWS, WIDTH)...  48.7 us
    unnamed x2, local copies, waits for them, and re-layouts  3.71 us

profile of v1, /device:TPU:1, one launch (start us, length us, event | category | flops | bytes accessed | tf_op | source)
XLA Modules:
  0.0 53.1 jit_solution(17558974657030500428)
XLA Ops:
  0.6 48.7 %shard_map.86 = (bf16[14,16,16]{2,1,0:T(8,128)(2,1)}, bf16[8,256,256]{2,1,0:T(8,128)(2,1)}) custom-call(s32[8,9]{1,0:T(8,128)} %links.1, bf16[14,16,16]{2,1,0:T(8,128)(2,1)} %top_sources.1, bf16[8,256,256]{2,1,0:T(8,128)(2,1)} %leaf_sources.1, bf16[14,16,256]{2,1,0:T(8,128)(2,1)} %top_inverse.1, bf16[8,256,256]{2,1,0:T(8,128)(2,1)} %leaf_inverse.1, ...), custom_call_target="tpu_custom_call" | custom-call | tf_op jit(solution)/shard_map/pallas_call | solution.py:316
  49.4 1.4 %copy.11 = bf16[14,16,16]{2,1,0:T(8,128)(2,1)} copy(bf16[14,16,16]{2,1,0:T(8,128)(2,1)} %get-tuple-element.4) | data formatting | bytes 14336
  50.8 2.3 %copy.12 = bf16[8,256,256]{2,1,0:T(8,128)(2,1)} copy(bf16[8,256,256]{2,1,0:T(8,128)(2,1)} %get-tuple-element.5) | data formatting | bytes 2097152

commit v2 on v1

--- a/solution.py
+++ b/solution.py
@@ -36,10 +36,12 @@
     leaf_inverse,
     top_coupling,
     leaf_coupling,
-    top_out,
-    leaf_out,
+    top_res,
+    leaf_res,
+    inverse,
     src_own,
     pack,
+    picks,
     zbuf,
     src_rows,
     sources,
@@ -53,18 +55,14 @@
     res_rows,
     residual,
     coupling,
-    inverse,
     leaf_src,
     update,
-    leaf_res,
-    top_res,
     local_sem,
     send_sem,
     recv_sem,
     core_send,
     core_recv,
     leaf_sem,
-    out_sem,
 ):
     col, row = lax.axis_index("col"), lax.axis_index("row")
     z, k = col // 2, lax.rem(col, 2)
@@ -92,7 +90,7 @@
 
     half0 = pl.ds(k, 1)
     half1 = pl.ds(LEVEL0 + 2 * k, 2)
-    half2 = pl.ds(EARLY + 4 * k, 4)
+    lanes = pl.ds(pl.multiple_of(k * HALF, HALF), HALF)
     pairs = pl.ds(2 * k, 2)
     early_pairs = pl.ds(0, LEVEL0)
     groups = (
@@ -102,7 +100,7 @@
             lambda at: coup1.at[pairs, :, at],
         ),
         (top_inverse.at[half1], lambda at: inv1.at[pairs, at]),
-        (top_inverse.at[half2], lambda at: inv2.at[pl.ds(4 * k, 4), at]),
+        (top_inverse.at[EARLY + z, :, lanes], lambda at: inv2.at[k, z, at]),
     )
     for g, (source, place) in enumerate(groups):
         pltpu.make_async_copy(source, place(rows), recv_sem.at[g]).start()
@@ -117,6 +115,12 @@
     place_lane = lax.broadcasted_iota(jnp.int32, (TOP * ROWS, BLOCK), 1) // WIDTH
     spread = jnp.where(place_row == place_lane, spread, 0.0)
     pack[...] = spread.reshape(TOP, ROWS, BLOCK).sum(axis=0).astype(BF16)
+
+    from_lane = lax.broadcasted_iota(jnp.int32, (HALF, HALF), 0)
+    to_lane = lax.broadcasted_iota(jnp.int32, (HALF, HALF), 1)
+    keep = from_lane // ROWS == to_lane // WIDTH
+    for j in range(8):
+        picks[j] = (from_lane == lax.rem(to_lane, WIDTH) + WIDTH * j).astype(F32).astype(BF16)
 
     pl.semaphore_wait(barrier, 2 * (PLANE - 1))
 
@@ -165,7 +169,7 @@
 
         lax.fori_loop(1, PLANE, send, 0)
 
-    for g in range(3):
+    for g in (3, 0, 1, 2):
         gather(g, groups[g][0], groups[g][1](rows))
 
     leaf_copies = (
@@ -177,26 +181,36 @@
         copy.start()
 
     pltpu.make_async_copy(zbuf, zbuf, recv_sem.at[4]).wait()
-    square = (HALF, HALF)
-    from_lane = lax.broadcasted_iota(jnp.int32, square, 0)
-    to_lane = lax.broadcasted_iota(jnp.int32, square, 1)
-    keep = from_lane // ROWS == to_lane // WIDTH
     collected = zbuf[...].reshape(HALF, BLOCK)
     for j in range(TOP):
-        pick = (from_lane == lax.rem(to_lane, WIDTH) + WIDTH * (j % 8)).astype(F32).astype(BF16)
-        moved = dot(collected[:, HALF * (j // 8) : HALF * (j // 8 + 1)], pick)
+        moved = dot(collected[:, HALF * (j // 8) : HALF * (j // 8 + 1)], picks[j % 8])
         moved = jnp.where(keep, moved, 0.0).reshape(DEPTH, ROWS, HALF).sum(axis=0).astype(BF16)
         src_rows[j] = moved
     early_rows = src_rows.at[pl.ds(0, EARLY)]
     pltpu.make_async_copy(early_rows, sources.at[:, rows], recv_sem.at[5]).start()
     gather(5, early_rows, sources.at[:, rows])
-    gather(3, groups[3][0], groups[3][1](rows))
+
+    mine = inv2.at[k, z]
+    pltpu.make_async_copy(mine, mine, recv_sem.at[3]).wait()
+
+    def send_inverse(d, carry):
+        pltpu.make_async_remote_copy(
+            src_ref=mine,
+            dst_ref=mine,
+            send_sem=send_sem.at[8],
+            recv_sem=recv_sem.at[7],
+            device_id=(lax.rem(z + d, DEPTH) * 2 + k, row),
+            device_id_type=MESH,
+        ).start()
+        return carry
+
+    lax.fori_loop(1, DEPTH, send_inverse, 0)
+    seven = inv2.at[k, pl.ds(0, DEPTH - 1)]
 
     halves = (
         inv0.at[half0],
         coup1.at[pairs],
         inv1.at[pairs],
-        inv2.at[pl.ds(4 * k, 4)],
     )
 
     def share(g, part):
@@ -223,57 +237,60 @@
     shared[1].wait_recv()
     shared[2].wait_recv()
     for j in range(LEVEL1):
-        total = dot(coup1[j, 0], early[k, 0]) + dot(coup1[j, 1], early[k, 1])
+        total = dot(
+            jnp.concatenate([coup1[j, 0], coup1[j, 1]], axis=1),
+            early[k, pl.ds(0, LEVEL0)].reshape(LEVEL0 * BLOCK, HALF),
+        )
         rest = (sources[LEVEL0 + j].astype(F32) - total).astype(BF16)
         early[k, LEVEL0 + j] = dot(inv1[j], rest).astype(BF16)
 
     second.wait()
-    total = jnp.zeros((LEVEL2 * ROWS, HALF), F32)
-    for b in range(EARLY):
-        total = total + dot(coup2[:, b].reshape(LEVEL2 * ROWS, BLOCK), early[k, b])
+    wide = [coup2[:, b].reshape(LEVEL2 * ROWS, BLOCK) for b in range(EARLY)]
+    total = dot(jnp.concatenate(wide, axis=1), early[k].reshape(EARLY * BLOCK, HALF))
     late_src = src_rows[pl.ds(EARLY, LEVEL2)].astype(F32)
     res_rows[...] = (late_src - total.reshape(LEVEL2, ROWS, HALF)).astype(BF16)
     pltpu.make_async_copy(res_rows, residual.at[:, rows], recv_sem.at[6]).start()
     gather(6, res_rows, residual.at[:, rows])
     shared.append(share(4, early.at[k]))
-    pltpu.make_async_copy(halves[3], halves[3], recv_sem.at[3]).wait()
-    shared.append(share(3, halves[3]))
 
     shared[3].wait_recv()
     for copy in leaf_copies:
         copy.wait()
 
     def early_leaf(i, carry):
-        total = leaf_src[i].astype(F32)
+        wide = jnp.concatenate([coupling[i, q] for q in range(EARLY_LINKS)], axis=1)
+        tall = []
         for q in range(EARLY_LINKS):
             at = links[i, q]
-            picked = jnp.concatenate([early[0, at], early[1, at]], axis=1)
-            total = total - dot(coupling[i, q], picked)
-        update[i] = total
+            tall.append(jnp.concatenate([early[0, at], early[1, at]], axis=1))
+        update[i] = leaf_src[i].astype(F32) - dot(wide, jnp.concatenate(tall, axis=0))
         return carry
 
     lax.fori_loop(0, LEAVES, early_leaf, 0)
+    pltpu.make_async_copy(seven, seven, recv_sem.at[7]).wait()
+    shared.append(share(3, inv2.at[k]))
 
     shared[4].wait_recv()
     pltpu.make_async_copy(residual, residual, recv_sem.at[6]).wait()
     for part in range(2):
         for j in range(4 * part, 4 * part + 4):
-            late[k, j] = dot(inv2[j], residual[j]).astype(BF16)
+            whole = jnp.concatenate([inv2[0, j], inv2[1, j]], axis=1)
+            late[k, j] = dot(whole, residual[j]).astype(BF16)
         shared.append(share(5 + part, late.at[k, pl.ds(4 * part, 4)]))
     shared[5].wait_recv()
     shared[6].wait_recv()
 
     def late_leaf(i, carry):
-        total = update[i]
+        wide = jnp.concatenate([coupling[i, q] for q in range(EARLY_LINKS, LINKS)], axis=1)
+        tall = []
         for q in range(EARLY_LINKS, LINKS):
             at = jnp.maximum(links[i, q] - EARLY, 0)
-            picked = jnp.concatenate([late[0, at], late[1, at]], axis=1)
-            total = total - dot(coupling[i, q], picked)
-        leaf_res[i] = dot(inverse[i], total.astype(BF16)).astype(BF16)
-        pltpu.make_async_copy(leaf_res.at[i], leaf_out.at[i], out_sem.at[0]).start()
+            tall.append(jnp.concatenate([late[0, at], late[1, at]], axis=1))
+        total = update[i] - dot(wide, jnp.concatenate(tall, axis=0))
+        leaf_res[i] = total.astype(BF16)
         return carry
 
-    lax.fori_loop(0, LEAVES, late_leaf, 0)
+    lax.fori_loop(0, LEAVES, late_leaf, 0, unroll=2)
 
     from_lane = lax.broadcasted_iota(jnp.int32, (HALF, WIDTH), 0)
     to_lane = lax.broadcasted_iota(jnp.int32, (HALF, WIDTH), 1)
@@ -282,8 +299,6 @@
     top_res[pl.ds(0, EARLY)] = dot(mine, pick).astype(BF16).reshape(EARLY, ROWS, WIDTH)
     mine = late[zhalf, :, rows].reshape(LEVEL2 * ROWS, HALF)
     top_res[pl.ds(EARLY, LEVEL2)] = dot(mine, pick).astype(BF16).reshape(LEVEL2, ROWS, WIDTH)
-    last = pltpu.make_async_copy(top_res, top_out, out_sem.at[1])
-    last.start()
 
     for copy in shared:
         copy.wait_send()
@@ -292,7 +307,7 @@
         inv0.at[half0, others],
         coup1.at[pairs, :, others],
         inv1.at[pairs, others],
-        inv2.at[pl.ds(4 * k, 4), others],
+        inv2.at[k, z, others],
         zbuf.at[pl.ds(0, DEPTH - 1)],
         sources.at[:, others],
         residual.at[:, others],
@@ -300,36 +315,48 @@
     for g, part in enumerate(sent):
         pltpu.make_async_copy(part, part, send_sem.at[g]).wait()
 
+    pltpu.make_async_copy(seven, seven, send_sem.at[8]).wait()
+
     @pl.when(k != zhalf)
     def _():
         pltpu.make_async_copy(pack, pack, send_sem.at[7]).wait()
 
-    pltpu.make_async_copy(leaf_res, leaf_out, out_sem.at[0]).wait()
+
+def finish(leaf_res, inverse, top_res, top_out, leaf_out, result, sem):
+    last = pltpu.make_async_copy(top_res, top_out, sem.at[1])
+    last.start()
+    for i in range(LEAVES):
+        result[i] = dot(inverse[i], leaf_res[i]).astype(BF16)
+        pltpu.make_async_copy(result.at[i], leaf_out.at[i], sem.at[0]).start()
+    pltpu.make_async_copy(result, leaf_out, sem.at[0]).wait()
     last.wait()
 
 
 def local(
     top_sources, leaf_sources, top_inverse, leaf_inverse, top_coupling, leaf_coupling, leaf_links
 ):
-    anywhere = pl.BlockSpec(memory_space=pl.ANY)
+    anywhere = pl.BlockSpec(memory_space=pltpu.HBM)
     vmem, dma = pltpu.VMEM, pltpu.SemaphoreType.DMA
-    return pl.pallas_call(
+    held = pl.BlockSpec(memory_space=vmem)
+    top_res, leaf_res, inverse = pl.pallas_call(
         kernel,
         out_shape=(
-            jax.ShapeDtypeStruct((TOP, ROWS, WIDTH), BF16),
-            jax.ShapeDtypeStruct((LEAVES, BLOCK, BLOCK), BF16),
+            vmem((TOP, ROWS, WIDTH), BF16),
+            vmem((LEAVES, BLOCK, BLOCK), BF16),
+            vmem((LEAVES, BLOCK, BLOCK), BF16),
         ),
         in_specs=[pl.BlockSpec(memory_space=pltpu.SMEM)] + [anywhere] * 6,
-        out_specs=(anywhere, anywhere),
+        out_specs=(held, held, held),
         scratch_shapes=[
             vmem((TOP, ROWS, WIDTH), BF16),
             vmem((ROWS, BLOCK), BF16),
+            vmem((8, HALF, HALF), BF16),
             vmem((DEPTH, ROWS, BLOCK), BF16),
             vmem((TOP, ROWS, HALF), BF16),
             vmem((EARLY, BLOCK, HALF), BF16),
             vmem((LEVEL0, BLOCK, BLOCK), BF16),
             vmem((LEVEL1, BLOCK, BLOCK), BF16),
-            vmem((LEVEL2, BLOCK, BLOCK), BF16),
+            vmem((2, LEVEL2, BLOCK, HALF), BF16),
             vmem((LEVEL1, LEVEL0, BLOCK, BLOCK), BF16),
             vmem((LEVEL2, EARLY, ROWS, BLOCK), BF16),
             vmem((2, EARLY, BLOCK, HALF), BF16),
@@ -338,20 +365,16 @@
             vmem((LEVEL2, BLOCK, HALF), BF16),
             vmem((LEAVES, LINKS, BLOCK, BLOCK), BF16),
             vmem((LEAVES, BLOCK, BLOCK), BF16),
-            vmem((LEAVES, BLOCK, BLOCK), BF16),
             vmem((LEAVES, BLOCK, BLOCK), F32),
-            vmem((LEAVES, BLOCK, BLOCK), BF16),
-            vmem((TOP, ROWS, WIDTH), BF16),
             dma((2,)),
+            dma((9,)),
             dma((8,)),
             dma((7,)),
             dma((7,)),
-            dma((7,)),
             dma((3,)),
-            dma((2,)),
         ],
         compiler_params=pltpu.CompilerParams(
-            collective_id=0, has_side_effects=True, vmem_limit_bytes=56 * 2**20
+            collective_id=0, has_side_effects=True, vmem_limit_bytes=59 * 2**20
         ),
     )(
         leaf_links,
@@ -362,6 +385,17 @@
         top_coupling,
         leaf_coupling,
     )
+    return pl.pallas_call(
+        finish,
+        out_shape=(
+            jax.ShapeDtypeStruct((TOP, ROWS, WIDTH), BF16),
+            jax.ShapeDtypeStruct((LEAVES, BLOCK, BLOCK), BF16),
+        ),
+        in_specs=[held] * 3,
+        out_specs=(anywhere, anywhere),
+        scratch_shapes=[vmem((LEAVES, BLOCK, BLOCK), BF16), dma((2,))],
+        compiler_params=pltpu.CompilerParams(vmem_limit_bytes=16 * 2**20),
+    )(leaf_res, inverse, top_res)
 
 
 def solution(mesh):

time: 53.9 us -> 46.2 us (0.86); the launches traced: 53.1 us -> 46 us
  local copies, waits for them, and re-layouts: 3.71 us -> 0 us
  Pallas kernels: 48.7 us -> 45.4 us
    unnamed x2 -> x0, local copies, waits for them, and re-layouts: 3.71 us -> none
    pallas_call x1 -> x2, Pallas kernels: 48.7 us -> 45.4 us  [the longest x1 44.2 us: local(): pl.pallas_call(kernel, out_shape=(vmem((TOP, ROWS, WIDTH), BF16), vmem((L...]
where the time goes in v2:
time: 46.2 us; the launch traced here: 46 us
  Pallas kernels  45.4 us (98%)
  between operations  0.64 us (1%)
    pallas_call x1, Pallas kernels, local(): pl.pallas_call(kernel, out_shape=(vmem((TOP, ROWS, WIDTH), BF16), vmem((L...  44.2 us
    pallas_call x1, Pallas kernels, local(): pl.pallas_call(finish, out_shape=(jax.ShapeDtypeStruct((TOP, ROWS, WIDTH)...  1.21 us

profile of v2, /device:TPU:1, one launch (start us, length us, event | category | flops | bytes accessed | tf_op | source)
XLA Modules:
  0.0 46.0 jit_solution(12732324389331086022)
XLA Ops:
  0.6 44.2 %shard_map.86 = (bf16[14,16,16]{2,1,0:T(8,128)(2,1)S(1)}, bf16[8,256,256]{2,1,0:T(8,128)(2,1)S(1)}, bf16[8,256,256]{2,1,0:T(8,128)(2,1)S(1)}) custom-call(s32[8,9]{1,0:T(8,128)} %links.1, bf16[14,16,16]{2,1,0:T(8,128)(2,1)} %top_sources.1, bf16[8,256,256]{2,1,0:T(8,128)(2,1)} %leaf_sources.1, bf16[14,16,256]{2,1,0:T(8,128)(2,1)} %top_inverse.1, ...), custom_call_target="tpu_custom_call" | custom-call | tf_op jit(solution)/shard_map/pallas_call | solution.py:341
  44.8 1.2 %shard_map.87 = (bf16[14,16,16]{2,1,0:T(8,128)(2,1)}, bf16[8,256,256]{2,1,0:T(8,128)(2,1)}) custom-call(bf16[8,256,256]{2,1,0:T(8,128)(2,1)S(1)} %get-tuple-element.5.leaf_res, bf16[8,256,256]{2,1,0:T(8,128)(2,1)S(1)} %get-tuple-element.6.inverse, bf16[14,16,16]{2,1,0:T(8,128)(2,1)S(1)} %get-tuple-element.7.top_res), custom_call_target="tpu_custom_call" | custom-call | tf_op jit(solution)/shard_map/pallas_call | solution.py:388

commit v3 on v2

--- a/solution.py
+++ b/solution.py
@@ -18,6 +18,7 @@
 ROWS = 16
 WIDTH = 16
 PLANE = 16
+SIDE = 4
 DEPTH = 8
 MESH = pl.DeviceIdType.MESH
 BF16 = jnp.bfloat16
@@ -69,6 +70,7 @@
     own = pl.multiple_of(row * ROWS, ROWS)
     rows = pl.ds(own, ROWS)
     other = (z * 2 + 1 - k, row)
+    x, y = row // SIDE, lax.rem(row, SIDE)
 
     def row_peer(d):
         return (col, lax.rem(row + d, PLANE))
@@ -97,7 +99,7 @@
         (top_inverse.at[half0], lambda at: inv0.at[half0, at]),
         (
             top_coupling.at[pairs, early_pairs],
-            lambda at: coup1.at[pairs, :, at],
+            lambda at: coup1.at[pairs, :, x, y],
         ),
         (top_inverse.at[half1], lambda at: inv1.at[pairs, at]),
         (top_inverse.at[EARLY + z, :, lanes], lambda at: inv2.at[k, z, at]),
@@ -155,7 +157,7 @@
 
     lax.fori_loop(1, DEPTH, send_z, 0)
 
-    def gather(g, source, target):
+    def gather_weights(g, source, target):
         def send(d, carry):
             pltpu.make_async_remote_copy(
                 src_ref=source,
@@ -169,8 +171,29 @@
 
         lax.fori_loop(1, PLANE, send, 0)
 
-    for g in (3, 0, 1, 2):
-        gather(g, groups[g][0], groups[g][1](rows))
+    def along(axis, g, r, source, target):
+        def send(d, carry):
+            peer = lax.rem(x + d, SIDE) * SIDE + y if axis == 0 else x * SIDE + lax.rem(y + d, SIDE)
+            pltpu.make_async_remote_copy(
+                src_ref=source,
+                dst_ref=target,
+                send_sem=send_sem.at[g],
+                recv_sem=recv_sem.at[r],
+                device_id=(col, peer),
+                device_id_type=MESH,
+            ).start()
+            return carry
+
+        lax.fori_loop(1, SIDE, send, 0)
+
+    for core in range(2):
+
+        @pl.when(k == core)
+        def _(core=core):
+            along(1 - core, 1, 1, groups[1][0], groups[1][1](rows))
+
+    for g in (3, 0, 2):
+        gather_weights(g, groups[g][0], groups[g][1](rows))
 
     leaf_copies = (
         pltpu.make_async_copy(leaf_sources, leaf_src, leaf_sem.at[0]),
@@ -180,15 +203,44 @@
     for copy in leaf_copies:
         copy.start()
 
+    for core in range(2):
+
+        @pl.when(k == core)
+        def _(core=core):
+            line = coup1.at[pairs, :, x] if core == 0 else coup1.at[pairs, :, :, y]
+            pltpu.make_async_copy(line, line, recv_sem.at[1]).wait()
+            along(core, 9, 8, line, line)
+
     pltpu.make_async_copy(zbuf, zbuf, recv_sem.at[4]).wait()
-    collected = zbuf[...].reshape(HALF, BLOCK)
-    for j in range(TOP):
-        moved = dot(collected[:, HALF * (j // 8) : HALF * (j // 8 + 1)], picks[j % 8])
-        moved = jnp.where(keep, moved, 0.0).reshape(DEPTH, ROWS, HALF).sum(axis=0).astype(BF16)
-        src_rows[j] = moved
-    early_rows = src_rows.at[pl.ds(0, EARLY)]
-    pltpu.make_async_copy(early_rows, sources.at[:, rows], recv_sem.at[5]).start()
-    gather(5, early_rows, sources.at[:, rows])
+
+    def unpack(start, stop):
+        collected = zbuf[...].reshape(HALF, BLOCK)
+        for j in range(start, stop):
+            moved = dot(collected[:, HALF * (j // 8) : HALF * (j // 8 + 1)], picks[j % 8])
+            moved = jnp.where(keep, moved, 0.0).reshape(DEPTH, ROWS, HALF).sum(axis=0)
+            src_rows[j] = moved.astype(BF16)
+
+    def gather(g, r, source, target):
+        pltpu.make_async_copy(source, target(rows), recv_sem.at[r]).start()
+
+        def send(d, carry):
+            pltpu.make_async_remote_copy(
+                src_ref=source,
+                dst_ref=target(rows),
+                send_sem=send_sem.at[g],
+                recv_sem=recv_sem.at[r],
+                device_id=row_peer(d),
+                device_id_type=MESH,
+            ).start()
+            return carry
+
+        lax.fori_loop(1, PLANE, send, 0)
+
+    level0, level1 = pl.ds(0, LEVEL0), pl.ds(LEVEL0, LEVEL1)
+    unpack(0, LEVEL0)
+    gather(5, 5, src_rows.at[level0], lambda at: sources.at[level0, at])
+    unpack(LEVEL0, EARLY)
+    gather(10, 9, src_rows.at[level1], lambda at: sources.at[level1, at])
 
     mine = inv2.at[k, z]
     pltpu.make_async_copy(mine, mine, recv_sem.at[3]).wait()
@@ -206,6 +258,7 @@
 
     lax.fori_loop(1, DEPTH, send_inverse, 0)
     seven = inv2.at[k, pl.ds(0, DEPTH - 1)]
+    unpack(EARLY, TOP)
 
     halves = (
         inv0.at[half0],
@@ -226,22 +279,27 @@
         return copy
 
     shared = []
-    for g in range(3):
-        pltpu.make_async_copy(halves[g], halves[g], recv_sem.at[g]).wait()
+    three = coup1.at[pairs, :, pl.ds(0, SIDE - 1)]
+    for g, r, part in ((0, 0, halves[0]), (1, 8, three), (2, 2, halves[2])):
+        pltpu.make_async_copy(part, part, recv_sem.at[r]).wait()
         shared.append(share(g, halves[g]))
 
     shared[0].wait_recv()
-    pltpu.make_async_copy(sources, sources, recv_sem.at[5]).wait()
+    part = sources.at[level0]
+    pltpu.make_async_copy(part, part, recv_sem.at[5]).wait()
     for b in range(LEVEL0):
         early[k, b] = dot(inv0[b], sources[b]).astype(BF16)
     shared[1].wait_recv()
+    totals = []
+    for j in range(LEVEL1):
+        wide = [coup1[j, b].reshape(BLOCK, BLOCK) for b in range(LEVEL0)]
+        tall = early[k, pl.ds(0, LEVEL0)].reshape(LEVEL0 * BLOCK, HALF)
+        totals.append(dot(jnp.concatenate(wide, axis=1), tall))
     shared[2].wait_recv()
+    part = sources.at[level1]
+    pltpu.make_async_copy(part, part, recv_sem.at[9]).wait()
     for j in range(LEVEL1):
-        total = dot(
-            jnp.concatenate([coup1[j, 0], coup1[j, 1]], axis=1),
-            early[k, pl.ds(0, LEVEL0)].reshape(LEVEL0 * BLOCK, HALF),
-        )
-        rest = (sources[LEVEL0 + j].astype(F32) - total).astype(BF16)
+        rest = (sources[LEVEL0 + j].astype(F32) - totals[j]).astype(BF16)
         early[k, LEVEL0 + j] = dot(inv1[j], rest).astype(BF16)
 
     second.wait()
@@ -249,11 +307,19 @@
     total = dot(jnp.concatenate(wide, axis=1), early[k].reshape(EARLY * BLOCK, HALF))
     late_src = src_rows[pl.ds(EARLY, LEVEL2)].astype(F32)
     res_rows[...] = (late_src - total.reshape(LEVEL2, ROWS, HALF)).astype(BF16)
-    pltpu.make_async_copy(res_rows, residual.at[:, rows], recv_sem.at[6]).start()
-    gather(6, res_rows, residual.at[:, rows])
+    chunks = (pl.ds(0, 4), pl.ds(4, 4))
+    for part, (g, r) in enumerate(((6, 6), (11, 10))):
+        chunk = chunks[part]
+        gather(g, r, res_rows.at[chunk], lambda at, chunk=chunk: residual.at[chunk, at])
     shared.append(share(4, early.at[k]))
 
     shared[3].wait_recv()
+
+    from_lane = lax.broadcasted_iota(jnp.int32, (HALF, WIDTH), 0)
+    to_lane = lax.broadcasted_iota(jnp.int32, (HALF, WIDTH), 1)
+    pick = (from_lane == to_lane + WIDTH * slot).astype(F32).astype(BF16)
+    first_rows = early[zhalf, :, rows].reshape(EARLY * ROWS, HALF)
+    top_res[pl.ds(0, EARLY)] = dot(first_rows, pick).astype(BF16).reshape(EARLY, ROWS, WIDTH)
     for copy in leaf_copies:
         copy.wait()
 
@@ -271,8 +337,9 @@
     shared.append(share(3, inv2.at[k]))
 
     shared[4].wait_recv()
-    pltpu.make_async_copy(residual, residual, recv_sem.at[6]).wait()
     for part in range(2):
+        chunk = residual.at[chunks[part]]
+        pltpu.make_async_copy(chunk, chunk, recv_sem.at[(6, 10)[part]]).wait()
         for j in range(4 * part, 4 * part + 4):
             whole = jnp.concatenate([inv2[0, j], inv2[1, j]], axis=1)
             late[k, j] = dot(whole, residual[j]).astype(BF16)
@@ -292,27 +359,25 @@
 
     lax.fori_loop(0, LEAVES, late_leaf, 0, unroll=2)
 
-    from_lane = lax.broadcasted_iota(jnp.int32, (HALF, WIDTH), 0)
-    to_lane = lax.broadcasted_iota(jnp.int32, (HALF, WIDTH), 1)
-    pick = (from_lane == to_lane + WIDTH * slot).astype(F32).astype(BF16)
-    mine = early[zhalf, :, rows].reshape(EARLY * ROWS, HALF)
-    top_res[pl.ds(0, EARLY)] = dot(mine, pick).astype(BF16).reshape(EARLY, ROWS, WIDTH)
-    mine = late[zhalf, :, rows].reshape(LEVEL2 * ROWS, HALF)
-    top_res[pl.ds(EARLY, LEVEL2)] = dot(mine, pick).astype(BF16).reshape(LEVEL2, ROWS, WIDTH)
+    rest = late[zhalf, :, rows].reshape(LEVEL2 * ROWS, HALF)
+    top_res[pl.ds(EARLY, LEVEL2)] = dot(rest, pick).astype(BF16).reshape(LEVEL2, ROWS, WIDTH)
 
     for copy in shared:
         copy.wait_send()
     others = pl.ds(0, BLOCK - ROWS)
     sent = (
-        inv0.at[half0, others],
-        coup1.at[pairs, :, others],
-        inv1.at[pairs, others],
-        inv2.at[k, z, others],
-        zbuf.at[pl.ds(0, DEPTH - 1)],
-        sources.at[:, others],
-        residual.at[:, others],
-    )
-    for g, part in enumerate(sent):
+        (0, inv0.at[half0, others]),
+        (1, coup1.at[pairs, :, 0, pl.ds(0, SIDE - 1)]),
+        (2, inv1.at[pairs, others]),
+        (3, inv2.at[k, z, others]),
+        (4, zbuf.at[pl.ds(0, DEPTH - 1)]),
+        (5, sources.at[level0, others]),
+        (6, residual.at[chunks[0], others]),
+        (9, three),
+        (10, sources.at[level1, others]),
+        (11, residual.at[chunks[1], others]),
+    )
+    for g, part in sent:
         pltpu.make_async_copy(part, part, send_sem.at[g]).wait()
 
     pltpu.make_async_copy(seven, seven, send_sem.at[8]).wait()
@@ -357,7 +422,7 @@
             vmem((LEVEL0, BLOCK, BLOCK), BF16),
             vmem((LEVEL1, BLOCK, BLOCK), BF16),
             vmem((2, LEVEL2, BLOCK, HALF), BF16),
-            vmem((LEVEL1, LEVEL0, BLOCK, BLOCK), BF16),
+            vmem((LEVEL1, LEVEL0, SIDE, SIDE, ROWS, BLOCK), BF16),
             vmem((LEVEL2, EARLY, ROWS, BLOCK), BF16),
             vmem((2, EARLY, BLOCK, HALF), BF16),
             vmem((2, LEVEL2, BLOCK, HALF), BF16),
@@ -367,8 +432,8 @@
             vmem((LEAVES, BLOCK, BLOCK), BF16),
             vmem((LEAVES, BLOCK, BLOCK), F32),
             dma((2,)),
-            dma((9,)),
-            dma((8,)),
+            dma((12,)),
+            dma((11,)),
             dma((7,)),
             dma((7,)),
             dma((3,)),

time: 46.2 us -> 43.6 us (0.944)
  Pallas kernels: 45.4 us -> 42.8 us
    pallas_call x1, Pallas kernels: 44.2 us -> 41.6 us  [local(): pl.pallas_call(kernel, out_shape=(vmem((TOP, ROWS, WIDTH), BF16), vmem((L...]
where the time goes in v3:
time: 43.6 us; the launch traced here: 43.4 us
  Pallas kernels  42.8 us (98%)
  between operations  0.64 us (1%)
    pallas_call x1, Pallas kernels, local(): pl.pallas_call(kernel, out_shape=(vmem((TOP, ROWS, WIDTH), BF16), vmem((L...  41.6 us
    pallas_call x1, Pallas kernels, local(): pl.pallas_call(finish, out_shape=(jax.ShapeDtypeStruct((TOP, ROWS, WIDTH)...  1.21 us

profile of v3, /device:TPU:1, one launch (start us, length us, event | category | flops | bytes accessed | tf_op | source)
XLA Modules:
  0.0 43.4 jit_solution(13078247210603337771)
XLA Ops:
  0.6 41.6 %shard_map.86 = (bf16[14,16,16]{2,1,0:T(8,128)(2,1)S(1)}, bf16[8,256,256]{2,1,0:T(8,128)(2,1)S(1)}, bf16[8,256,256]{2,1,0:T(8,128)(2,1)S(1)}) custom-call(s32[8,9]{1,0:T(8,128)} %links.1, bf16[14,16,16]{2,1,0:T(8,128)(2,1)} %top_sources.1, bf16[8,256,256]{2,1,0:T(8,128)(2,1)} %leaf_sources.1, bf16[14,16,256]{2,1,0:T(8,128)(2,1)} %top_inverse.1, ...), custom_call_target="tpu_custom_call" | custom-call | tf_op jit(solution)/shard_map/pallas_call | solution.py:406
  42.2 1.2 %shard_map.87 = (bf16[14,16,16]{2,1,0:T(8,128)(2,1)}, bf16[8,256,256]{2,1,0:T(8,128)(2,1)}) custom-call(bf16[8,256,256]{2,1,0:T(8,128)(2,1)S(1)} %get-tuple-element.5.leaf_res, bf16[8,256,256]{2,1,0:T(8,128)(2,1)S(1)} %get-tuple-element.6.inverse, bf16[14,16,16]{2,1,0:T(8,128)(2,1)S(1)} %get-tuple-element.7.top_res), custom_call_target="tpu_custom_call" | custom-call | tf_op jit(solution)/shard_map/pallas_call | solution.py:453

commit v4 on v3

--- a/solution.py
+++ b/solution.py
@@ -101,7 +101,7 @@
             top_coupling.at[pairs, early_pairs],
             lambda at: coup1.at[pairs, :, x, y],
         ),
-        (top_inverse.at[half1], lambda at: inv1.at[pairs, at]),
+        (top_inverse.at[half1], lambda at: inv1.at[pairs, x, y]),
         (top_inverse.at[EARLY + z, :, lanes], lambda at: inv2.at[k, z, at]),
     )
     for g, (source, place) in enumerate(groups):
@@ -191,8 +191,9 @@
         @pl.when(k == core)
         def _(core=core):
             along(1 - core, 1, 1, groups[1][0], groups[1][1](rows))
-
-    for g in (3, 0, 2):
+            along(1 - core, 2, 2, groups[2][0], groups[2][1](rows))
+
+    for g in (3, 0):
         gather_weights(g, groups[g][0], groups[g][1](rows))
 
     leaf_copies = (
@@ -210,6 +211,9 @@
             line = coup1.at[pairs, :, x] if core == 0 else coup1.at[pairs, :, :, y]
             pltpu.make_async_copy(line, line, recv_sem.at[1]).wait()
             along(core, 9, 8, line, line)
+            line = inv1.at[pairs, x] if core == 0 else inv1.at[pairs, :, y]
+            pltpu.make_async_copy(line, line, recv_sem.at[2]).wait()
+            along(core, 12, 11, line, line)
 
     pltpu.make_async_copy(zbuf, zbuf, recv_sem.at[4]).wait()
 
@@ -280,7 +284,8 @@
 
     shared = []
     three = coup1.at[pairs, :, pl.ds(0, SIDE - 1)]
-    for g, r, part in ((0, 0, halves[0]), (1, 8, three), (2, 2, halves[2])):
+    three_inv = inv1.at[pairs, pl.ds(0, SIDE - 1)]
+    for g, r, part in ((0, 0, halves[0]), (1, 8, three), (2, 11, three_inv)):
         pltpu.make_async_copy(part, part, recv_sem.at[r]).wait()
         shared.append(share(g, halves[g]))
 
@@ -300,7 +305,7 @@
     pltpu.make_async_copy(part, part, recv_sem.at[9]).wait()
     for j in range(LEVEL1):
         rest = (sources[LEVEL0 + j].astype(F32) - totals[j]).astype(BF16)
-        early[k, LEVEL0 + j] = dot(inv1[j], rest).astype(BF16)
+        early[k, LEVEL0 + j] = dot(inv1[j].reshape(BLOCK, BLOCK), rest).astype(BF16)
 
     second.wait()
     wide = [coup2[:, b].reshape(LEVEL2 * ROWS, BLOCK) for b in range(EARLY)]
@@ -357,7 +362,7 @@
         leaf_res[i] = total.astype(BF16)
         return carry
 
-    lax.fori_loop(0, LEAVES, late_leaf, 0, unroll=2)
+    lax.fori_loop(0, LEAVES, late_leaf, 0, unroll=LEAVES)
 
     rest = late[zhalf, :, rows].reshape(LEVEL2 * ROWS, HALF)
     top_res[pl.ds(EARLY, LEVEL2)] = dot(rest, pick).astype(BF16).reshape(LEVEL2, ROWS, WIDTH)
@@ -368,7 +373,8 @@
     sent = (
         (0, inv0.at[half0, others]),
         (1, coup1.at[pairs, :, 0, pl.ds(0, SIDE - 1)]),
-        (2, inv1.at[pairs, others]),
+        (2, inv1.at[pairs, 0, pl.ds(0, SIDE - 1)]),
+        (12, three_inv),
         (3, inv2.at[k, z, others]),
         (4, zbuf.at[pl.ds(0, DEPTH - 1)]),
         (5, sources.at[level0, others]),
@@ -420,7 +426,7 @@
             vmem((TOP, ROWS, HALF), BF16),
             vmem((EARLY, BLOCK, HALF), BF16),
             vmem((LEVEL0, BLOCK, BLOCK), BF16),
-            vmem((LEVEL1, BLOCK, BLOCK), BF16),
+            vmem((LEVEL1, SIDE, SIDE, ROWS, BLOCK), BF16),
             vmem((2, LEVEL2, BLOCK, HALF), BF16),
             vmem((LEVEL1, LEVEL0, SIDE, SIDE, ROWS, BLOCK), BF16),
             vmem((LEVEL2, EARLY, ROWS, BLOCK), BF16),
@@ -432,8 +438,8 @@
             vmem((LEAVES, BLOCK, BLOCK), BF16),
             vmem((LEAVES, BLOCK, BLOCK), F32),
             dma((2,)),
+            dma((13,)),
             dma((12,)),
-            dma((11,)),
             dma((7,)),
             dma((7,)),
             dma((3,)),

time: 43.6 us -> 41.6 us (0.954)
  Pallas kernels: 42.8 us -> 40.8 us
    pallas_call x1, Pallas kernels: 41.6 us -> 39.6 us  [local(): pl.pallas_call(kernel, out_shape=(vmem((TOP, ROWS, WIDTH), BF16), vmem((L...]
where the time goes in v4:
time: 41.6 us; the launch traced here: 41.5 us
  Pallas kernels  40.8 us (98%)
  between operations  0.64 us (2%)
    pallas_call x1, Pallas kernels, local(): pl.pallas_call(kernel, out_shape=(vmem((TOP, ROWS, WIDTH), BF16), vmem((L...  39.6 us
    pallas_call x1, Pallas kernels, local(): pl.pallas_call(finish, out_shape=(jax.ShapeDtypeStruct((TOP, ROWS, WIDTH)...  1.21 us

profile of v4, /device:TPU:1, one launch (start us, length us, event | category | flops | bytes accessed | tf_op | source)
XLA Modules:
  0.0 41.5 jit_solution(17420911365223776833)
XLA Ops:
  0.6 39.6 %shard_map.86 = (bf16[14,16,16]{2,1,0:T(8,128)(2,1)S(1)}, bf16[8,256,256]{2,1,0:T(8,128)(2,1)S(1)}, bf16[8,256,256]{2,1,0:T(8,128)(2,1)S(1)}) custom-call(s32[8,9]{1,0:T(8,128)} %links.1, bf16[14,16,16]{2,1,0:T(8,128)(2,1)} %top_sources.1, bf16[8,256,256]{2,1,0:T(8,128)(2,1)} %leaf_sources.1, bf16[14,16,256]{2,1,0:T(8,128)(2,1)} %top_inverse.1, ...), custom_call_target="tpu_custom_call" | custom-call | tf_op jit(solution)/shard_map/pallas_call | solution.py:412
  40.3 1.2 %shard_map.87 = (bf16[14,16,16]{2,1,0:T(8,128)(2,1)}, bf16[8,256,256]{2,1,0:T(8,128)(2,1)}) custom-call(bf16[8,256,256]{2,1,0:T(8,128)(2,1)S(1)} %get-tuple-element.5.leaf_res, bf16[8,256,256]{2,1,0:T(8,128)(2,1)S(1)} %get-tuple-element.6.inverse, bf16[14,16,16]{2,1,0:T(8,128)(2,1)S(1)} %get-tuple-element.7.top_res), custom_call_target="tpu_custom_call" | custom-call | tf_op jit(solution)/shard_map/pallas_call | solution.py:459
